TPU v7x, 32 devices: a whole 2x2x4 slice. The times are simulated.
32 devices in a mesh: grp: 2 (over y), seq: 4 (over z), head: 2 (over x), sub: 2 (over core).
Axes of the slice: x: 2, y: 2, z: 4, core: 2. Of those that a mesh axis runs over, the one named last changes fastest.
Arguments:
- q_mant: bfloat16 [1024, 6144], P(('grp', 'seq', 'head', 'sub')), parts along dimension 0, may hold values from -4 to 4
- q_exp: int32 [1024, 48], P(('grp', 'seq', 'head', 'sub')), parts along dimension 0, may hold values from -2 to 1
- text_kv: bfloat16 [2, 1024, 6144], P(None, 'grp', ('head', 'sub')), parts along dimension 1, may hold values from -4 to 4
- out_weight: bfloat16 [6144, 6144], P(('head', 'sub'), 'seq'), may hold values from -0.3125 to 0.3125
- lengths: int32 [8], P('grp'), parts along dimension 0, may hold values from 64 to 512, as said below
Outputs:
- mixed: bfloat16 [1024, 6144], P(('grp', 'seq', 'head', 'sub')), parts along dimension 0
There are 2 independent parts, one for each index of `grp`. A program takes and returns all parts, laid end to end along the dimension named above; an argument that names none is the same for every part. Nothing has to cross between parts.
Inputs may be any that keep to these rules, and one draw needn't show every extreme that they name: `lengths`: some frame sees all 512 text tokens.
All inputs are finite; a program needn't handle non-finite values.
Results may differ from a plain program's by a relative error of at most 0.009.
Values may be sent and summed in bfloat16 or wider, within the bound.
A program may use at most 128 MiB of HBM per device.

v0:
```python
import jax
import jax.numpy as jnp
from jax import lax
from jax.sharding import PartitionSpec as P

FRAME_TOK = 128


def shards(q_mant, q_exp, text_kv, out_weight, lengths):
    tok_dev = q_mant.shape[0]
    heads_all = q_exp.shape[1]
    n_head = lax.axis_size("head")
    n_sub = lax.axis_size("sub")
    groups = n_head * n_sub
    local_heads = heads_all // groups
    head_size = q_mant.shape[1] // heads_all
    rows = tok_dev * groups
    mantissa, expo = (
        lax.all_to_all(q_mant, ("head", "sub"), split_axis=1, concat_axis=0, tiled=True),
        lax.all_to_all(q_exp, ("head", "sub"), split_axis=1, concat_axis=0, tiled=True),
    )
    factor = jnp.exp2(expo.astype(jnp.float32))
    query = (
        mantissa.reshape(rows, local_heads, head_size).astype(jnp.float32) * factor[:, :, None]
    ).astype(jnp.bfloat16)
    keys = text_kv[0].reshape(-1, local_heads, head_size)
    values = text_kv[1].reshape(-1, local_heads, head_size)
    text_len = keys.shape[0]
    frames = lengths.shape[0]
    row_index = lax.axis_index("seq") * rows + jnp.arange(rows, dtype=jnp.int32)
    frame = row_index // FRAME_TOK
    limit = jnp.sum(
        jnp.where(
            frame[:, None] == jnp.arange(frames, dtype=jnp.int32)[None, :], lengths[None, :], 0
        ),
        axis=1,
    )
    valid = jnp.arange(text_len, dtype=jnp.int32)[None, :] < limit[:, None]
    scores = jnp.einsum("rhd,thd->hrt", query, keys, preferred_element_type=jnp.float32) * (
        1.0 / head_size**0.5
    )
    scores = jnp.where(valid[None], scores, -1e30)
    top = jnp.max(scores, axis=2, keepdims=True)
    probs = jnp.where(valid[None], jnp.exp(scores - top), 0.0)
    total = jnp.sum(probs, axis=2, keepdims=True)
    weights = (probs / total).astype(jnp.bfloat16)
    attended = jnp.einsum(
        "hrt,thd->rhd", weights, values, preferred_element_type=jnp.float32
    ).astype(jnp.bfloat16)
    attended = attended.reshape(rows, local_heads * head_size)
    term = jnp.dot(
        attended,
        lax.all_gather(out_weight, "seq", axis=1, tiled=True),
        preferred_element_type=jnp.float32,
    )
    summed = lax.psum_scatter(
        term.astype(jnp.bfloat16), ("head", "sub"), scatter_dimension=0, tiled=True
    )
    return summed


def solution(mesh):
    return jax.shard_map(
        shards,
        mesh=mesh,
        in_specs=(
            P(("grp", "seq", "head", "sub"), None),
            P(("grp", "seq", "head", "sub"), None),
            P(None, "grp", ("head", "sub")),
            P(("head", "sub"), "seq"),
            P("grp"),
        ),
        out_specs=P(("grp", "seq", "head", "sub"), None),
        check_vma=False,
    )
```

profile of v0, /device:TPU:0, one launch (start us, length us, event | category | flops | bytes accessed | tf_op | source)
XLA Modules:
  0.0 378.5 jit_solution(7905054542764979671)
XLA Ops:
  6.5 0.0 copy-start.2
  6.5 0.0 all-gather.2.cloned.1.call-start
  6.5 0.7 all-gather.2.cloned.1.call-update
  7.3 0.0 copy-done.2
  7.3 0.1 copy.16
  7.4 0.7 reshape.66
  8.0 4.2 %all-to-all-start.1 = ((s32[4,1,384]{2,1,0:T(1,128)}), s32[4,1,384]{2,1,0:T(1,128)S(1)}, u32[]{:S(2)}, u32[]{:S(2)}) async-start(s32[4,1,384]{2,1,0:T(1,128)} %reshape.66), calls=%async_computation.1 | async-start | bytes 12288 | tf_op jit(solution)/shard_map/all_to_all | solution.py:20
  12.2 0.0 copy-start.3
  12.3 0.0 copy-start.1
  12.3 3.3 fusion.11
  15.6 0.0 copy-done.3
  15.6 0.1 select_reduce_fusion
  15.6 0.0 copy-done.1
  15.6 0.8 copy.31
  16.4 0.0 all-to-all-done.1
  16.4 4.1 %all-to-all-start = ((bf16[32,4,1536]{2,0,1:T(8,128)(2,1)}), bf16[32,4,1536]{2,0,1:T(8,128)(2,1)}, u32[]{:S(2)}, u32[]{:S(2)}) async-start(bf16[32,4,1536]{2,0,1:T(8,128)(2,1)} %bitcast.22), calls=%async_computation | async-start | bytes 786432 | tf_op jit(solution)/shard_map/all_to_all | solution.py:19
  20.6 0.0 reduce-scatter.2.cloned.1.call-start
  20.6 0.1 iota_compare_fusion
  20.7 2.0 copy.26
  22.8 1.6 copy.22
  24.3 0.6 broadcast.59
  24.9 0.7 reduce
  25.6 0.1 reshape.67
  25.7 0.1 copy.24
  25.8 2.3 all-to-all-done
  28.1 1.1 convert_bitcast_fusion
  29.2 0.1 reshape.65
  29.3 0.3 multiply_convert_fusion
  29.7 0.6 fusion.7
  30.2 0.0 copy-start
  30.3 1.5 fusion.12
  31.8 0.0 copy-done
  31.8 0.7 fusion.6
  32.5 301.7 %all-gather.2.cloned.1.call-done = bf16[1536,6144]{1,0:T(8,128)(2,1)} async-done(((bf16[1536,1536]{1,0:T(8,128)(2,1)}), bf16[1536,6144]{1,0:T(8,128)(2,1)}) %all-gather.2.cloned.1.call-update) | async-done | bytes 18874384 | tf_op jit(solution)/shard_map/all_gather | solution.py:53
  334.3 10.2 %convolution_convert_fusion = bf16[128,6144]{1,0:T(8,128)(2,1)} fusion(bf16[128,1536]{0,1:T(8,128)(2,1)S(1)} %bitcast.25, bf16[1536,6144]{1,0:T(8,128)(2,1)} %all-gather.2.cloned.1.call-done), kind=kOutput, calls=%fused_computation.1 | convolution fusion | flops 2416705536 | bytes 20840448 | tf_op jit(solution)/shard_map/dot_general | solution.py:51
  344.5 0.0 reduce-scatter.2.cloned.1.call-update
  344.5 27.2 %reduce-scatter.2.cloned.1.call-done = bf16[32,6144]{1,0:T(8,128)(2,1)} async-done(((bf16[128,6144]{1,0:T(8,128)(2,1)}), bf16[32,6144]{1,0:T(8,128)(2,1)}) %reduce-scatter.2.cloned.1.call-update) | async-done | bytes 393232 | tf_op jit(solution)/shard_map/reduce_scatter | solution.py:56
  (3 shorter events, 0.0 us)
Async XLA Ops:
  6.5 0.7 copy-start.2
  6.5 327.7 %all-gather.2.cloned.1.call-start = ((), (), s32[]{:S(2)}) async-start(), calls=%async_computation.3 | async-start | bytes 23592960 | tf_op jit(solution)/shard_map/all_gather | solution.py:53
  8.0 8.4 %all-to-all-start.1 = ((s32[4,1,384]{2,1,0:T(1,128)}), s32[4,1,384]{2,1,0:T(1,128)S(1)}, u32[]{:S(2)}, u32[]{:S(2)}) async-start(s32[4,1,384]{2,1,0:T(1,128)} %reshape.66), calls=%async_computation.1 | async-start | bytes 12288 | tf_op jit(solution)/shard_map/all_to_all | solution.py:20
  12.2 3.3 copy-start.3
  12.3 3.4 copy-start.1
  16.4 11.7 %all-to-all-start = ((bf16[32,4,1536]{2,0,1:T(8,128)(2,1)}), bf16[32,4,1536]{2,0,1:T(8,128)(2,1)}, u32[]{:S(2)}, u32[]{:S(2)}) async-start(bf16[32,4,1536]{2,0,1:T(8,128)(2,1)} %bitcast.22), calls=%async_computation | async-start | bytes 786432 | tf_op jit(solution)/shard_map/all_to_all | solution.py:19
  20.6 351.1 %reduce-scatter.2.cloned.1.call-start = ((), (), s32[]{:S(2)}) async-start(), calls=%async_computation.4 | async-start | bytes 1966080 | tf_op jit(solution)/shard_map/reduce_scatter | solution.py:56
  30.2 1.6 copy-start
Sparse Core Ops, SparseCore 0:
  8.9 325.2 all-gather.1
  344.7 26.9 reduce-scatter.1
where the time goes:
time: 379 us
  waiting for transfers between devices  332 us (88%)
  between operations  13.5 us (4%)
  matrix products  11.5 us (3%)
  local copies, waits for them, and re-layouts  9.36 us (2%)
  starting transfers between devices  8.38 us (2%)
  other arithmetic  3.89 us (1%)
    all_gather x1, waiting for transfers between devices, shards(): lax.all_gather(out_weight, 'seq', axis=1, tiled=True)  302 us
    reduce_scatter x1, waiting for transfers between devices, shards(): lax.psum_scatter(term.astype(jnp.bfloat16), ('head', 'sub'), scatter_dime...  27.2 us
    dot_general x1, matrix products, shards(): jnp.dot(attended, lax.all_gather(out_weight, 'seq', axis=1, tiled=True),...  10.2 us
  transfers between devices with their start and end apart: 4, of which 3 were waited for; matrix products, arithmetic and copies ran while one was open for 4% of the time, Pallas kernels for 0%

commit v1 on v0

--- a/solution.py
+++ b/solution.py
@@ -9,20 +9,19 @@
 def shards(q_mant, q_exp, text_kv, out_weight, lengths):
     tok_dev = q_mant.shape[0]
     heads_all = q_exp.shape[1]
-    n_head = lax.axis_size("head")
-    n_sub = lax.axis_size("sub")
-    groups = n_head * n_sub
+    groups = lax.axis_size("head") * lax.axis_size("sub")
+    seq = lax.axis_size("seq")
     local_heads = heads_all // groups
     head_size = q_mant.shape[1] // heads_all
     rows = tok_dev * groups
-    mantissa, expo = (
-        lax.all_to_all(q_mant, ("head", "sub"), split_axis=1, concat_axis=0, tiled=True),
-        lax.all_to_all(q_exp, ("head", "sub"), split_axis=1, concat_axis=0, tiled=True),
+    factor = jnp.exp2(q_exp.astype(jnp.float32))
+    query = (
+        q_mant.reshape(tok_dev, heads_all, head_size).astype(jnp.float32) * factor[:, :, None]
+    ).astype(jnp.bfloat16)
+    query = lax.all_to_all(
+        query.reshape(q_mant.shape), ("head", "sub"), split_axis=1, concat_axis=0, tiled=True
     )
-    factor = jnp.exp2(expo.astype(jnp.float32))
-    query = (
-        mantissa.reshape(rows, local_heads, head_size).astype(jnp.float32) * factor[:, :, None]
-    ).astype(jnp.bfloat16)
+    query = query.reshape(rows, local_heads, head_size)
     keys = text_kv[0].reshape(-1, local_heads, head_size)
     values = text_kv[1].reshape(-1, local_heads, head_size)
     text_len = keys.shape[0]
@@ -48,15 +47,19 @@
         "hrt,thd->rhd", weights, values, preferred_element_type=jnp.float32
     ).astype(jnp.bfloat16)
     attended = attended.reshape(rows, local_heads * head_size)
+    gathered = lax.all_gather(attended, "seq", axis=0, tiled=False)
     term = jnp.dot(
-        attended,
-        lax.all_gather(out_weight, "seq", axis=1, tiled=True),
-        preferred_element_type=jnp.float32,
+        gathered.reshape(seq * rows, -1), out_weight, preferred_element_type=jnp.float32
+    ).astype(jnp.bfloat16)
+    cols = term.shape[1]
+    term = term.reshape(seq, groups, tok_dev, cols).transpose(1, 0, 2, 3)
+    summed = lax.psum_scatter(
+        term.reshape(groups * seq * tok_dev, cols), ("head", "sub"), scatter_dimension=0, tiled=True
     )
-    summed = lax.psum_scatter(
-        term.astype(jnp.bfloat16), ("head", "sub"), scatter_dimension=0, tiled=True
+    mixed = lax.all_to_all(
+        summed.reshape(seq, tok_dev, cols), "seq", split_axis=0, concat_axis=0, tiled=True
     )
-    return summed
+    return mixed.transpose(1, 0, 2).reshape(tok_dev, seq * cols)
 
 
 def solution(mesh):

time: 379 us -> 123 us (0.32)
  waiting for transfers between devices: 332 us -> 66.9 us
  blocking collectives: 0 us -> 16.3 us
  matrix products: 11.5 us -> 6.68 us
  starting transfers between devices: 8.38 us -> 4.25 us
    all_gather x1, waiting for transfers between devices: 302 us -> 39 us  [shards(): gathered = lax.all_gather(attended, 'seq', axis=0, tiled=False)]
    all_to_all x0 -> x1, blocking collectives: none -> 16.3 us  [shards(): lax.all_to_all(summed.reshape(seq, tok_dev, cols), 'seq', split_axis=0, c...]
    dot_general x1, matrix products: 10.2 us -> 5.41 us  [shards(): jnp.dot(gathered.reshape(seq * rows, -1), out_weight, preferred_element_t...]
    all_to_all x2 -> x1, starting transfers between devices: 8.34 us -> 4.21 us  [shards(): lax.all_to_all(query.reshape(q_mant.shape), ('head', 'sub'), split_axis=1...]
  transfers between devices with their start and end apart: 4 -> 3, of which waited for: 3 -> 3; matrix products, arithmetic and copies ran while one was open for 4% -> 6% of each run, Pallas kernels for 0% -> 0%
where the time goes in v1:
time: 123 us; the launch traced here: 122 us
  waiting for transfers between devices  66.9 us (54%)
  blocking collectives  16.3 us (13%)
  between operations  13.5 us (11%)
  local copies, waits for them, and re-layouts  10.9 us (9%)
  matrix products  6.68 us (5%)
  starting transfers between devices  4.25 us (3%)
  other arithmetic  3.72 us (3%)
    all_gather x1, waiting for transfers between devices, shards(): gathered = lax.all_gather(attended, 'seq', axis=0, tiled=False)  39 us
    reduce_scatter x1, waiting for transfers between devices, shards(): lax.psum_scatter(term.reshape(groups * seq * tok_dev, cols), ('head', 'su...  27.2 us
    all_to_all x1, blocking collectives, shards(): lax.all_to_all(summed.reshape(seq, tok_dev, cols), 'seq', split_axis=0, c...  16.3 us
    dot_general x1, matrix products, shards(): jnp.dot(gathered.reshape(seq * rows, -1), out_weight, preferred_element_t...  5.41 us
    all_to_all x1, starting transfers between devices, shards(): lax.all_to_all(query.reshape(q_mant.shape), ('head', 'sub'), split_axis=1...  4.21 us
    slice x1, local copies, waits for them, and re-layouts, shards(): keys = text_kv[0].reshape(-1, local_heads, head_size)  3.24 us
  transfers between devices with their start and end apart: 3, of which 3 were waited for; matrix products, arithmetic and copies ran while one was open for 6% of the time, Pallas kernels for 0%

profile of v1, /device:TPU:0, one launch (start us, length us, event | category | flops | bytes accessed | tf_op | source)
XLA Modules:
  0.0 122.2 jit_solution(10045359775647328987)
XLA Ops:
  6.5 0.7 multiply_exponential_fusion
  7.3 0.3 mul.21
  7.5 1.3 %fusion.7 = bf16[32,6144]{1,0:T(8,128)(2,1)S(1)} fusion(f32[4,8,48,128]{3,2,1,0:T(8,128)S(1)} %bitcast.30, bf16[32,6144]{1,0:T(8,128)(2,1)} %param.5), kind=kLoop, calls=%fused_computation.12 | loop fusion | flops 589824 | bytes 1572864 | tf_op jit(solution)/shard_map/convert_element_type | solution.py:20
  8.8 0.8 copy.47
  9.6 4.2 %all-to-all-start = ((bf16[32,4,1536]{2,0,1:T(8,128)(2,1)}), bf16[32,4,1536]{2,0,1:T(8,128)(2,1)S(1)}, u32[]{:S(2)}, u32[]{:S(2)}) async-start(bf16[32,4,1536]{2,0,1:T(8,128)(2,1)} %bitcast.27), calls=%async_computation | async-start | bytes 786432 | tf_op jit(solution)/shard_map/all_to_all | solution.py:21
  13.8 0.0 all-gather.2.cloned.1.call-start
  13.8 3.2 %fusion.12 = (bf16[1,512,1536]{2,1,0:T(8,128)(2,1)}, bf16[1,512,1536]{2,1,0:T(8,128)(2,1)S(1)}) fusion(bf16[2,512,1536]{2,1,0:T(8,128)(2,1)} %param.7), kind=kLoop, calls=%fused_computation.26 | loop fusion | bytes 6291456 | tf_op jit(solution)/shard_map/slice | solution.py:25
  17.0 0.0 copy-start.1
  17.0 1.7 %copy.39 = bf16[1,512,1536]{1,2,0:T(8,128)(2,1)S(1)} copy(bf16[1,512,1536]{2,1,0:T(8,128)(2,1)} %get-tuple-element.5) | data formatting | bytes 3145728
  18.8 1.6 %copy.34 = bf16[1,512,1536]{1,2,0:T(8,128)(2,1)} copy(bf16[1,512,1536]{2,1,0:T(8,128)(2,1)S(1)} %get-tuple-element.6) | data formatting | bytes 3145728 | tf_op jit(solution)/shard_map/slice | solution.py:26
  20.4 0.0 copy-done.1
  20.4 0.1 select_reduce_fusion
  20.4 0.1 iota_compare_fusion
  20.6 0.6 all-to-all-done
  21.2 0.3 reshape.66
  21.5 0.6 fusion.8
  22.0 0.0 copy-start
  22.1 1.5 %fusion.13 = (f32[12,128]{1,0:T(8,128)S(1)}, f32[12,128,512]{2,1,0:T(8,128)S(1)}) fusion(f32[12,128,512]{2,1,0:T(8,128)S(1)} %fusion.8, pred[128,512]{1,0:T(8,128)(4,1)S(1)} %iota_compare_fusion), kind=kOutput, calls=%fused_computation.27 | output fusion | flops 5505535 | bytes 6363136 | tf_op jit(solution)/shard_map/sub | solution.py:43
  23.6 0.0 copy-done
  23.6 0.7 fusion.6
  24.3 0.9 copy.35
  25.3 0.0 all-gather.2.cloned.1.call-update
  25.3 0.0 reduce-scatter.2.cloned.1.call-start
  25.3 39.0 %all-gather.2.cloned.1.call-done = bf16[4,128,1536]{2,1,0:T(8,128)(2,1)} async-done(((bf16[1,128,1536]{2,1,0:T(8,128)(2,1)}), bf16[4,128,1536]{2,1,0:T(8,128)(2,1)}) %all-gather.2.cloned.1.call-update) | async-done | bytes 1572880 | tf_op jit(solution)/shard_map/all_gather | solution.py:50
  64.3 5.4 %convolution_convert_fusion = bf16[512,1536]{1,0:T(8,128)(2,1)S(1)} fusion(bf16[512,1536]{1,0:T(8,128)(2,1)} %bitcast.38, bf16[1536,1536]{1,0:T(8,128)(2,1)} %param.8), kind=kOutput, calls=%fused_computation.4 | convolution fusion | flops 2416705536 | bytes 7864320 | tf_op jit(solution)/shard_map/dot_general | solution.py:51
  69.8 1.3 %copy.36 = bf16[4,4,32,1536]{3,2,0,1:T(8,128)(2,1)} copy(bf16[4,4,32,1536]{3,2,1,0:T(8,128)(2,1)S(1)} %bitcast.32) | data formatting | bytes 3145728 | tf_op jit(solution)/shard_map/reshape | solution.py:55
  71.1 0.0 reduce-scatter.2.cloned.1.call-update
  71.1 27.2 %reduce-scatter.2.cloned.1.call-done = bf16[128,1536]{1,0:T(8,128)(2,1)} async-done(((bf16[512,1536]{1,0:T(8,128)(2,1)}), bf16[128,1536]{1,0:T(8,128)(2,1)}) %reduce-scatter.2.cloned.1.call-update) | async-done | bytes 393232 | tf_op jit(solution)/shard_map/reduce_scatter | solution.py:56
  98.3 16.3 %all_to_all.21 = bf16[4,32,1536]{2,1,0:T(8,128)(2,1)S(1)} all-to-all(bf16[4,32,1536]{2,1,0:T(8,128)(2,1)} %bitcast.36), channel_id=1, replica_groups=mesh['grp'=2,'seq'=4,'head'=2,'sub'=2] {'seq'}, dimensions={0} | all-to-all | bytes 786432 | tf_op jit(solution)/shard_map/all_to_all | solution.py:59
  114.5 0.8 copy.41
  (1 shorter events, 0.0 us)
Async XLA Ops:
  9.6 11.7 %all-to-all-start = ((bf16[32,4,1536]{2,0,1:T(8,128)(2,1)}), bf16[32,4,1536]{2,0,1:T(8,128)(2,1)S(1)}, u32[]{:S(2)}, u32[]{:S(2)}) async-start(bf16[32,4,1536]{2,0,1:T(8,128)(2,1)} %bitcast.27), calls=%async_computation | async-start | bytes 786432 | tf_op jit(solution)/shard_map/all_to_all | solution.py:21
  13.8 50.6 %all-gather.2.cloned.1.call-start = ((), (), s32[]{:S(2)}) async-start(), calls=%async_computation.3 | async-start | bytes 1966080 | tf_op jit(solution)/shard_map/all_gather | solution.py:50
  17.0 3.3 %copy-start.1 = (s32[4]{0:T(128)S(1)}, s32[4]{0:T(128)}, u32[]{:S(2)}) copy-start(s32[4]{0:T(128)} %param.9) | copy-start | bytes 52
  22.0 1.6 %copy-start = (bf16[1,512,1536]{1,2,0:T(8,128)(2,1)S(1)}, bf16[1,512,1536]{1,2,0:T(8,128)(2,1)}, u32[]{:S(2)}) copy-start(bf16[1,512,1536]{1,2,0:T(8,128)(2,1)} %copy.34) | copy-start | bytes 4718596
  25.3 73.0 %reduce-scatter.2.cloned.1.call-start = ((), (), s32[]{:S(2)}) async-start(), calls=%async_computation.4 | async-start | bytes 1966080 | tf_op jit(solution)/shard_map/reduce_scatter | solution.py:56
Sparse Core Ops, SparseCore 0:
  25.4 38.9 all-gather.1
  71.2 27.0 reduce-scatter.1

commit v2 on v1

--- a/solution.py
+++ b/solution.py
@@ -1,9 +1,372 @@
+import functools
+import math
+
 import jax
 import jax.numpy as jnp
 from jax import lax
+from jax.experimental import pallas as pl
+from jax.experimental.pallas import tpu as pltpu
 from jax.sharding import PartitionSpec as P
 
 FRAME_TOK = 128
+MESH = pl.DeviceIdType.MESH
+CHUNKS = 2
+PARTS = 2
+BLOCK = 512
+UNROLL = 3
+
+
+def kernel(
+    dims, q_ref, e_ref, len_ref, kv_ref, w_ref, out_ref,
+    kv, w, qs, qr, att, part, sib, y, rx, done,
+    load_sem, q_send, q_recv, att_send, att_recv, sib_send, sib_recv,
+    x_send, x_recv, out_send, out_recv,
+):
+    seq, n_head, n_sub, heads_all = dims
+    groups = n_head * n_sub
+    head_size = q_ref.shape[1] // heads_all
+    width = w_ref.shape[0]
+    cols = w_ref.shape[1]
+    local_heads = width // head_size
+    text_len = kv_ref.shape[1]
+    tok = q_ref.shape[0] // CHUNKS
+    rows = groups * tok
+    part_width = width // PARTS
+    part_heads = local_heads // PARTS
+    z, h, u = lax.axis_index("seq"), lax.axis_index("head"), lax.axis_index("sub")
+    me = h * n_sub + u
+    f32, bf16 = jnp.float32, jnp.bfloat16
+
+    loads = [
+        pltpu.make_async_copy(kv_ref.at[0], kv.at[0], load_sem.at[0]),
+        pltpu.make_async_copy(kv_ref.at[1], kv.at[1], load_sem.at[1]),
+        pltpu.make_async_copy(w_ref, w, load_sem.at[2]),
+    ]
+    for load in loads:
+        load.start()
+
+    def owner_id(step):
+        peer = lax.rem(me + step, groups)
+        return {"head": peer // n_sub, "sub": lax.rem(peer, n_sub)}
+
+    barrier = pltpu.get_barrier_semaphore()
+    for step in range(1, groups):
+        pl.semaphore_signal(barrier, inc=1, device_id=owner_id(step), device_id_type=MESH)
+    for step in range(1, seq):
+        pl.semaphore_signal(
+            barrier, inc=1, device_id={"seq": lax.rem(z + step, seq)}, device_id_type=MESH
+        )
+
+    factor = jnp.exp2(e_ref[...].astype(f32))
+    for one in range(heads_all):
+        group, local = one // local_heads, one % local_heads
+        block = q_ref[:, one * head_size:(one + 1) * head_size].astype(f32)
+        block = (block * factor[:, one:one + 1]).astype(bf16)
+        for j in range(CHUNKS):
+            qs[j, group, :, local * head_size:(local + 1) * head_size] = block[j * tok:(j + 1) * tok]
+
+    pl.semaphore_wait(barrier, groups - 1 + seq - 1)
+
+    def q_copy(j, step):
+        return pltpu.make_async_remote_copy(
+            src_ref=qs.at[j, lax.rem(me + step, groups)],
+            dst_ref=qr.at[j, me],
+            send_sem=q_send.at[j, step],
+            recv_sem=q_recv.at[j, step],
+            device_id=owner_id(step),
+            device_id_type=MESH,
+        )
+
+    for j in range(CHUNKS):
+        for step in range(1, groups):
+            q_copy(j, step).start()
+    for j in range(CHUNKS):
+        qr[j, me] = qs[j, me]
+
+    def att_copy(way, k, t):
+        block = z - t if way == 0 else z + t
+        place = att.at[k, jnp.clip(block, 0, seq - 1)]
+        return pltpu.make_async_remote_copy(
+            src_ref=place,
+            dst_ref=place,
+            send_sem=att_send.at[way, k, t],
+            recv_sem=att_recv.at[way, k, t],
+            device_id={"seq": z + 1 if way == 0 else z - 1},
+            device_id_type=MESH,
+        )
+
+    def can_send(way, t):
+        return (z - t >= 0) & (z + 1 < seq) if way == 0 else (z + t < seq) & (z - 1 >= 0)
+
+    def can_take(way, t):
+        return z - t >= 0 if way == 0 else z + t < seq
+
+    def arrive(k, t):
+        for way in range(2):
+
+            @pl.when(can_take(way, t))
+            def _():
+                block = z - t if way == 0 else z + t
+                place = att.at[k, jnp.clip(block, 0, seq - 1)]
+                pltpu.make_async_remote_copy(
+                    src_ref=place,
+                    dst_ref=place,
+                    send_sem=att_send.at[way, k, t - 1],
+                    recv_sem=att_recv.at[way, k, t - 1],
+                    device_id={"seq": z - 1 if way == 0 else z + 1},
+                    device_id_type=MESH,
+                ).wait_recv()
+
+            if t < seq - 1:
+
+                @pl.when(can_send(way, t))
+                def _():
+                    att_copy(way, k, t).start()
+
+    rows_seq = q_ref.shape[0] * groups
+    limit = len_ref[(z * rows_seq) // FRAME_TOK]
+    valid = lax.broadcasted_iota(jnp.int32, (rows, text_len), 1) < limit
+    scale = math.log2(math.e) / head_size**0.5
+
+    def attend(k):
+        j, c = k // PARTS, k % PARTS
+
+        def some(i, carry):
+            for extra in range(UNROLL):
+                inner = pl.multiple_of((i * UNROLL + extra) * head_size, head_size)
+                outer = pl.multiple_of(c * part_width + inner, head_size)
+                query = qr[j, :, :, pl.ds(outer, head_size)].reshape(rows, head_size)
+                keys = kv[0, :, pl.ds(outer, head_size)]
+                values = kv[1, :, pl.ds(outer, head_size)]
+                scores = lax.dot_general(
+                    query, keys, (((1,), (1,)), ((), ())), preferred_element_type=f32
+                )
+                scores = jnp.where(valid, scores, -1e30)
+                top = jnp.max(scores, axis=1, keepdims=True)
+                probs = jnp.exp2((scores - top) * scale)
+                total = jnp.sum(probs, axis=1, keepdims=True)
+                mixed = jnp.dot(probs.astype(bf16), values, preferred_element_type=f32)
+                att[k, z, :, pl.ds(inner, head_size)] = (mixed * (1.0 / total)).astype(bf16)
+            return carry
+
+        lax.fori_loop(0, part_heads // UNROLL, some, 0)
+        for way in range(2):
+
+            @pl.when(can_send(way, 0))
+            def _():
+                att_copy(way, k, 0).start()
+
+    half = seq // 2
+
+    def first_of(i):
+        own = z // half
+        return (own if i == 0 else 1 - own) * half
+
+    def sib_copy(j, i):
+        place = pl.ds(first_of(i), half)
+        return pltpu.make_async_remote_copy(
+            src_ref=part.at[j, place, 1 - u],
+            dst_ref=sib.at[j, place],
+            send_sem=sib_send.at[j, i],
+            recv_sem=sib_recv.at[j, i],
+            device_id={"sub": 1 - u},
+            device_id_type=MESH,
+        )
+
+    def project(j, i):
+        place = pl.ds(first_of(i), half)
+
+        def block(n, carry):
+            lanes = pl.ds(pl.multiple_of(n * BLOCK, BLOCK), BLOCK)
+            term = None
+            for c in range(PARTS):
+                left = att[j * PARTS + c, place].reshape(half * rows, part_width)
+                more = jnp.dot(
+                    left, w[c * part_width:(c + 1) * part_width, lanes], preferred_element_type=f32
+                )
+                term = more if term is None else term + more
+            term = term.astype(bf16).reshape(half, n_head, n_sub, tok, BLOCK)
+            for sub in range(n_sub):
+                part[j, place, sub, :, :, lanes] = term[:, :, sub]
+            return carry
+
+        lax.fori_loop(0, cols // BLOCK, block, 0)
+        sib_copy(j, i).start()
+
+    def x_copy(j, i):
+        place = pl.ds(first_of(i), half)
+        return pltpu.make_async_remote_copy(
+            src_ref=y.at[j, place],
+            dst_ref=rx.at[j, place],
+            send_sem=x_send.at[j, i],
+            recv_sem=x_recv.at[j, i],
+            device_id={"head": 1 - h},
+            device_id_type=MESH,
+        )
+
+    def pair(j, i):
+        place = pl.ds(first_of(i), half)
+        sib_copy(j, i).wait_recv()
+        y[j, place] = (
+            part[j, place, u, 1 - h].astype(f32) + sib[j, place, 1 - h].astype(f32)
+        ).astype(bf16)
+        x_copy(j, i).start()
+
+    lanes_out = pl.ds(pl.multiple_of(z * cols, cols), cols)
+
+    def out_copy(j, target):
+        return pltpu.make_async_remote_copy(
+            src_ref=done.at[j, target],
+            dst_ref=out_ref.at[pl.ds(j * tok, tok), lanes_out],
+            send_sem=out_send.at[j, target],
+            recv_sem=out_recv.at[j, z],
+            device_id={"seq": target},
+            device_id_type=MESH,
+        )
+
+    def finish(j, i):
+        place = pl.ds(first_of(i), half)
+        x_copy(j, i).wait_recv()
+        done[j, place] = (
+            part[j, place, u, h].astype(f32) + sib[j, place, h].astype(f32) + rx[j, place].astype(f32)
+        ).astype(bf16)
+        for one in range(half):
+            target = first_of(i) + one
+
+            @pl.when(target != z)
+            def _():
+                out_copy(j, target).start()
+
+        if i == 0:
+            out_ref[pl.ds(j * tok, tok), lanes_out] = done[j, z]
+
+    loads[0].wait()
+    loads[1].wait()
+
+    def q_ready(j):
+        for step in range(1, groups):
+            q_copy(j, step).wait_recv()
+
+    q_ready(0)
+    attend(0)
+    attend(1)
+    arrive(0, 1)
+    q_ready(1)
+    attend(2)
+    arrive(1, 1)
+    arrive(0, 2)
+    attend(3)
+    arrive(2, 1)
+    arrive(1, 2)
+    loads[2].wait()
+    project(0, 0)
+    arrive(3, 1)
+    arrive(2, 2)
+    arrive(0, 3)
+    arrive(1, 3)
+    project(0, 1)
+    arrive(3, 2)
+    pair(0, 0)
+    project(1, 0)
+    pair(0, 1)
+    finish(0, 0)
+    pair(1, 0)
+    finish(0, 1)
+    arrive(2, 3)
+    arrive(3, 3)
+    project(1, 1)
+    finish(1, 0)
+    pair(1, 1)
+    finish(1, 1)
+
+    for j in range(CHUNKS):
+        for source in range(seq):
+
+            @pl.when(source != z)
+            def _():
+                pltpu.make_async_remote_copy(
+                    src_ref=done.at[j, source],
+                    dst_ref=out_ref.at[pl.ds(j * tok, tok), source * cols:(source + 1) * cols],
+                    send_sem=out_send.at[j, source],
+                    recv_sem=out_recv.at[j, source],
+                    device_id={"seq": source},
+                    device_id_type=MESH,
+                ).wait_recv()
+                out_copy(j, source).wait_send()
+
+        for step in range(1, groups):
+            q_copy(j, step).wait_send()
+        for i in range(2):
+            sib_copy(j, i).wait_send()
+            x_copy(j, i).wait_send()
+    for way in range(2):
+        for k in range(CHUNKS * PARTS):
+            for t in range(seq - 1):
+
+                @pl.when(can_send(way, t))
+                def _():
+                    att_copy(way, k, t).wait_send()
+
+
+def fused(mesh, q_mant, q_exp, text_kv, out_weight, lengths):
+    seq, n_head, n_sub = mesh.shape["seq"], mesh.shape["head"], mesh.shape["sub"]
+    groups = n_head * n_sub
+    tok = q_mant.shape[0] // CHUNKS
+    width, cols = out_weight.shape
+    items = CHUNKS * PARTS
+    bf16 = jnp.bfloat16
+    dma = pltpu.SemaphoreType.DMA
+    return pl.pallas_call(
+        functools.partial(kernel, (seq, n_head, n_sub, q_exp.shape[1])),
+        out_shape=jax.ShapeDtypeStruct(q_mant.shape, bf16),
+        in_specs=[
+            pl.BlockSpec(memory_space=pltpu.VMEM),
+            pl.BlockSpec(memory_space=pltpu.VMEM),
+            pl.BlockSpec(memory_space=pltpu.SMEM),
+            pl.BlockSpec(memory_space=pl.ANY),
+            pl.BlockSpec(memory_space=pl.ANY),
+        ],
+        out_specs=pl.BlockSpec(memory_space=pltpu.VMEM),
+        scratch_shapes=[
+            pltpu.VMEM(text_kv.shape, bf16),
+            pltpu.VMEM(out_weight.shape, bf16),
+            pltpu.VMEM((CHUNKS, groups, tok, width), bf16),
+            pltpu.VMEM((CHUNKS, groups, tok, width), bf16),
+            pltpu.VMEM((items, seq, groups * tok, width // PARTS), bf16),
+            pltpu.VMEM((CHUNKS, seq, n_sub, n_head, tok, cols), bf16),
+            pltpu.VMEM((CHUNKS, seq, n_head, tok, cols), bf16),
+            pltpu.VMEM((CHUNKS, seq, tok, cols), bf16),
+            pltpu.VMEM((CHUNKS, seq, tok, cols), bf16),
+            pltpu.VMEM((CHUNKS, seq, tok, cols), bf16),
+            dma((3,)),
+            dma((CHUNKS, groups)),
+            dma((CHUNKS, groups)),
+            dma((2, items, seq)),
+            dma((2, items, seq)),
+            dma((CHUNKS, 2)),
+            dma((CHUNKS, 2)),
+            dma((CHUNKS, 2)),
+            dma((CHUNKS, 2)),
+            dma((CHUNKS, seq)),
+            dma((CHUNKS, seq)),
+        ],
+        compiler_params=pltpu.CompilerParams(
+            collective_id=0, has_side_effects=True, vmem_limit_bytes=56 * 2**20
+        ),
+    )(q_mant, q_exp, lengths, text_kv, out_weight)
+
+
+def fits(mesh, q_mant, q_exp, text_kv, out_weight, lengths):
+    if (mesh.shape["seq"], mesh.shape["head"], mesh.shape["sub"]) != (4, 2, 2):
+        return False
+    head_size = q_mant.shape[1] // q_exp.shape[1]
+    return (
+        head_size == 128
+        and q_mant.shape[0] * 4 == FRAME_TOK
+        and q_mant.shape[0] % (16 * CHUNKS) == 0
+        and (out_weight.shape[0] // head_size) % (PARTS * UNROLL) == 0
+        and out_weight.shape[1] % BLOCK == 0
+    )
 
 
 def shards(q_mant, q_exp, text_kv, out_weight, lengths):
@@ -63,8 +426,11 @@
 
 
 def solution(mesh):
+    def step(*arrays):
+        return fused(mesh, *arrays) if fits(mesh, *arrays) else shards(*arrays)
+
     return jax.shard_map(
-        shards,
+        step,
         mesh=mesh,
         in_specs=(
             P(("grp", "seq", "head", "sub"), None),

time: 123 us -> 55.6 us (0.45)
  waiting for transfers between devices: 66.9 us -> 0 us
  Pallas kernels: 0 us -> 53.7 us
  blocking collectives: 16.3 us -> 0 us
  between operations: 13.5 us -> 0.01 us
  local copies, waits for them, and re-layouts: 10.9 us -> 1.77 us
  matrix products: 6.68 us -> 0 us
  starting transfers between devices: 4.25 us -> 0 us
  other arithmetic: 3.72 us -> 0 us
    pallas_call x0 -> x1, Pallas kernels: none -> 53.7 us  [fused(): pl.pallas_call(functools.partial(kernel, (seq, n_head, n_sub, q_exp.shape...]
    all_gather x1 -> x0, waiting for transfers between devices: 39 us -> none  [shards(): gathered = lax.all_gather(attended, 'seq', axis=0, tiled=False)]
    reduce_scatter x1 -> x0, waiting for transfers between devices: 27.2 us -> none  [shards(): lax.psum_scatter(term.reshape(groups * seq * tok_dev, cols), ('head', 'su...]
    all_to_all x1 -> x0, blocking collectives: 16.3 us -> none  [shards(): lax.all_to_all(summed.reshape(seq, tok_dev, cols), 'seq', split_axis=0, c...]
    dot_general x3 -> x0, matrix products: 6.68 us -> none  [the longest x1 5.41 us: shards(): jnp.dot(gathered.reshape(seq * rows, -1), out_weight, preferred_element_t...]
    slice x2 -> x0, local copies, waits for them, and re-layouts: 4.84 us -> none  [the longest x1 3.24 us: shards(): keys = text_kv[0].reshape(-1, local_heads, head_size)]
    all_to_all x1 -> x0, starting transfers between devices: 4.21 us -> none  [shards(): lax.all_to_all(query.reshape(q_mant.shape), ('head', 'sub'), split_axis=1...]
    reshape x3 -> x0, local copies, waits for them, and re-layouts: 2.34 us -> none  [the longest x1 1.29 us: shards(): term = term.reshape(seq, groups, tok_dev, cols).transpose(1, 0, 2, 3)]
  transfers between devices with their start and end apart: 3 -> 0, of which waited for: 3 -> 0; matrix products, arithmetic and copies ran while one was open for 6% -> 0% of each run, Pallas kernels for 0% -> 0%
where the time goes in v2:
time: 55.6 us; the launch traced here: 55.5 us
  Pallas kernels  53.7 us (97%)
  local copies, waits for them, and re-layouts  1.77 us (3%)
    pallas_call x1, Pallas kernels, fused(): pl.pallas_call(functools.partial(kernel, (seq, n_head, n_sub, q_exp.shape...  53.7 us
    unnamed x1, local copies, waits for them, and re-layouts  1.77 us

profile of v2, /device:TPU:0, one launch (start us, length us, event | category | flops | bytes accessed | tf_op | source)
XLA Modules:
  0.0 55.5 jit_solution(10773171255731403305)
XLA Ops:
  0.0 53.7 %shard_map.55 = bf16[32,6144]{1,0:T(8,128)(2,1)} custom-call(bf16[32,6144]{1,0:T(8,128)(2,1)} %q_ref.1, s32[32,48]{1,0:T(8,128)} %e_ref.1, s32[4]{0:T(128)} %len_ref.1, bf16[2,512,1536]{2,1,0:T(8,128)(2,1)} %kv_ref.1, bf16[1536,1536]{1,0:T(8,128)(2,1)} %w_ref.1), custom_call_target="tpu_custom_call" | custom-call | tf_op jit(solution)/shard_map/pallas_call | solution.py:319
  53.7 1.8 %copy.7 = bf16[32,6144]{1,0:T(8,128)(2,1)} copy(bf16[32,6144]{1,0:T(8,128)(2,1)} %shard_map.55) | data formatting | bytes 786432

commit v3 on v1

--- a/solution.py
+++ b/solution.py
@@ -1,9 +1,335 @@
+import functools
+import math
+
 import jax
 import jax.numpy as jnp
 from jax import lax
+from jax.experimental import pallas as pl
+from jax.experimental.pallas import tpu as pltpu
 from jax.sharding import PartitionSpec as P
 
 FRAME_TOK = 128
+MESH = pl.DeviceIdType.MESH
+BLOCK = 512
+UNROLL = 4
+
+
+def kernel(
+    dims, q_ref, e_ref, len_ref, kv_ref, w_ref, out_ref,
+    kv, w, qs, qr, att, part, sib, y, rx, done,
+    load_sem, q_send, q_recv, att_send, att_recv, sib_send, sib_recv,
+    x_send, x_recv, out_send, out_recv,
+):
+    seq, n_head, n_sub, heads_all = dims
+    groups = n_head * n_sub
+    head_size = q_ref.shape[1] // heads_all
+    width, cols = w_ref.shape
+    local_heads = width // head_size
+    text_len = kv_ref.shape[1]
+    rows = q_ref.shape[0]
+    z, h, u = lax.axis_index("seq"), lax.axis_index("head"), lax.axis_index("sub")
+    me = h * n_sub + u
+    f32, bf16 = jnp.float32, jnp.bfloat16
+
+    loads = [
+        pltpu.make_async_copy(kv_ref.at[0], kv.at[0], load_sem.at[0]),
+        pltpu.make_async_copy(kv_ref.at[1], kv.at[1], load_sem.at[1]),
+        pltpu.make_async_copy(w_ref, w, load_sem.at[2]),
+    ]
+    for load in loads:
+        load.start()
+
+    def owner(d):
+        return (h if d < 2 else 1 - h), (u if d % 2 == 0 else 1 - u)
+
+    def owner_id(d):
+        head, sub = owner(d)
+        return {"head": head, "sub": sub}
+
+    barrier = pltpu.get_barrier_semaphore()
+    for d in range(1, groups):
+        pl.semaphore_signal(barrier, inc=1, device_id=owner_id(d), device_id_type=MESH)
+    for step in range(1, seq):
+        pl.semaphore_signal(
+            barrier, inc=1, device_id={"seq": lax.rem(z + step, seq)}, device_id_type=MESH
+        )
+
+    factor = jnp.exp2(e_ref[...].astype(f32))
+    for one in range(heads_all):
+        group, local = one // local_heads, one % local_heads
+        block = q_ref[:, one * head_size:(one + 1) * head_size].astype(f32)
+        block = (block * factor[:, one:one + 1]).astype(bf16)
+        qs[group, :, local * head_size:(local + 1) * head_size] = block
+
+    pl.semaphore_wait(barrier, groups - 1 + seq - 1)
+
+    def q_copy(d):
+        head, sub = owner(d)
+        return pltpu.make_async_remote_copy(
+            src_ref=qs.at[head * n_sub + sub],
+            dst_ref=qr.at[d],
+            send_sem=q_send.at[d],
+            recv_sem=q_recv.at[d],
+            device_id=owner_id(d),
+            device_id_type=MESH,
+        )
+
+    for d in (2, 3, 1):
+        q_copy(d).start()
+    qr[0] = qs[me]
+
+    def block_of(way, t):
+        return jnp.clip(z - t if way == 0 else z + t, 0, seq - 1)
+
+    def att_copy(way, t, d, target):
+        place = att.at[block_of(way, t), d]
+        sem = t if target else t - 1
+        return pltpu.make_async_remote_copy(
+            src_ref=place,
+            dst_ref=place,
+            send_sem=att_send.at[way, sem, d],
+            recv_sem=att_recv.at[way, sem, d],
+            device_id={"seq": z + 1 if (way == 0) == target else z - 1},
+            device_id_type=MESH,
+        )
+
+    def can_send(way, t):
+        return (z - t >= 0) & (z + 1 < seq) if way == 0 else (z + t < seq) & (z - 1 >= 0)
+
+    def can_take(way, t):
+        return z - t >= 0 if way == 0 else z + t < seq
+
+    def arrive(t, d):
+        for way in range(2):
+
+            @pl.when(can_take(way, t))
+            def _():
+                att_copy(way, t, d, False).wait_recv()
+
+            if t < seq - 1:
+
+                @pl.when(can_send(way, t))
+                def _():
+                    att_copy(way, t, d, True).start()
+
+    limit = len_ref[(z * rows * groups) // FRAME_TOK]
+    valid = lax.broadcasted_iota(jnp.int32, (rows, text_len), 1) < limit
+    scale = math.log2(math.e) / head_size**0.5
+
+    def attend(d):
+        def some(i, carry):
+            for extra in range(UNROLL):
+                lanes = pl.ds(pl.multiple_of((i * UNROLL + extra) * head_size, head_size), head_size)
+                scores = lax.dot_general(
+                    qr[d, :, lanes], kv[0, :, lanes], (((1,), (1,)), ((), ())),
+                    preferred_element_type=f32,
+                )
+                scores = jnp.where(valid, scores, -1e30)
+                top = jnp.max(scores, axis=1, keepdims=True)
+                probs = jnp.exp2((scores - top) * scale)
+                total = jnp.sum(probs, axis=1, keepdims=True)
+                mixed = jnp.dot(probs.astype(bf16), kv[1, :, lanes], preferred_element_type=f32)
+                att[z, d, :, lanes] = (mixed * (1.0 / total)).astype(bf16)
+            return carry
+
+        lax.fori_loop(0, local_heads // UNROLL, some, 0)
+        for way in range(2):
+
+            @pl.when(can_send(way, 0))
+            def _():
+                att_copy(way, 0, d, True).start()
+
+    last = jnp.where(z < 2, 3, 0)
+    second = 1 + lax.rem(z, 2)
+    order = (z, second, 6 - z - second - last, last)
+
+    def sib_copy(p, far):
+        return pltpu.make_async_remote_copy(
+            src_ref=part.at[order[p], 2 * far + 1],
+            dst_ref=sib.at[order[p], far],
+            send_sem=sib_send.at[p, far],
+            recv_sem=sib_recv.at[p, far],
+            device_id={"sub": 1 - u},
+            device_id_type=MESH,
+        )
+
+    def project(p, first, count):
+        def block(n, carry):
+            lanes = pl.ds(pl.multiple_of(n * BLOCK, BLOCK), BLOCK)
+            left = att[order[p], first:first + count].reshape(count * rows, width)
+            term = jnp.dot(left, w[:, lanes], preferred_element_type=f32)
+            part[order[p], first:first + count, :, lanes] = term.astype(bf16).reshape(
+                count, rows, BLOCK
+            )
+            return carry
+
+        lax.fori_loop(0, cols // BLOCK, block, 0)
+        if first + count == groups:
+            sib_copy(p, 1).start()
+        if first == 0:
+            sib_copy(p, 0).start()
+
+    def x_copy(p):
+        return pltpu.make_async_remote_copy(
+            src_ref=y.at[order[p]],
+            dst_ref=rx.at[order[p]],
+            send_sem=x_send.at[p],
+            recv_sem=x_recv.at[p],
+            device_id={"head": 1 - h},
+            device_id_type=MESH,
+        )
+
+    def pair(p):
+        place = order[p]
+        sib_copy(p, 1).wait_recv()
+        y[place] = (part[place, 2].astype(f32) + sib[place, 1].astype(f32)).astype(bf16)
+        x_copy(p).start()
+
+    lanes_out = pl.ds(pl.multiple_of(z * cols, cols), cols)
+
+    def out_copy(p):
+        return pltpu.make_async_remote_copy(
+            src_ref=done.at[order[p]],
+            dst_ref=out_ref.at[:, lanes_out],
+            send_sem=out_send.at[p],
+            recv_sem=out_recv.at[z],
+            device_id={"seq": order[p]},
+            device_id_type=MESH,
+        )
+
+    def finish(p):
+        place = order[p]
+        sib_copy(p, 0).wait_recv()
+        x_copy(p).wait_recv()
+        total = part[place, 0].astype(f32) + sib[place, 0].astype(f32) + rx[place].astype(f32)
+        if p == 0:
+            out_ref[:, lanes_out] = total.astype(bf16)
+        else:
+            done[place] = total.astype(bf16)
+            out_copy(p).start()
+
+    loads[0].wait()
+    loads[1].wait()
+    attend(0)
+    q_copy(1).wait_recv()
+    attend(1)
+    arrive(1, 0)
+    q_copy(2).wait_recv()
+    attend(2)
+    arrive(1, 1)
+    q_copy(3).wait_recv()
+    attend(3)
+    arrive(1, 2)
+    loads[2].wait()
+    project(0, 0, 4)
+    arrive(1, 3)
+    pair(0)
+    project(1, 0, 4)
+    pair(1)
+    for d in (2, 3, 0, 1):
+        arrive(2, d)
+    finish(1)
+    project(2, 0, 4)
+    pair(2)
+    finish(2)
+    arrive(3, 2)
+    arrive(3, 3)
+    project(3, 2, 2)
+    pair(3)
+    arrive(3, 0)
+    arrive(3, 1)
+    project(3, 0, 2)
+    finish(0)
+    finish(3)
+
+    for source in range(seq):
+
+        @pl.when(source != z)
+        def _():
+            pltpu.make_async_remote_copy(
+                src_ref=done.at[source],
+                dst_ref=out_ref.at[:, source * cols:(source + 1) * cols],
+                send_sem=out_send.at[0],
+                recv_sem=out_recv.at[source],
+                device_id={"seq": source},
+                device_id_type=MESH,
+            ).wait_recv()
+
+    for d in range(1, groups):
+        q_copy(d).wait_send()
+    for p in range(seq):
+        sib_copy(p, 0).wait_send()
+        sib_copy(p, 1).wait_send()
+        x_copy(p).wait_send()
+        if p:
+            out_copy(p).wait_send()
+    for way in range(2):
+        for t in range(seq - 1):
+            for d in range(groups):
+
+                @pl.when(can_send(way, t))
+                def _():
+                    att_copy(way, t, d, True).wait_send()
+
+
+def fused(mesh, q_mant, q_exp, text_kv, out_weight, lengths):
+    seq, n_head, n_sub = mesh.shape["seq"], mesh.shape["head"], mesh.shape["sub"]
+    groups = n_head * n_sub
+    rows = q_mant.shape[0]
+    width, cols = out_weight.shape
+    bf16 = jnp.bfloat16
+    dma = pltpu.SemaphoreType.DMA
+    return pl.pallas_call(
+        functools.partial(kernel, (seq, n_head, n_sub, q_exp.shape[1])),
+        out_shape=jax.ShapeDtypeStruct(q_mant.shape, bf16),
+        in_specs=[
+            pl.BlockSpec(memory_space=pltpu.VMEM),
+            pl.BlockSpec(memory_space=pltpu.VMEM),
+            pl.BlockSpec(memory_space=pltpu.SMEM),
+            pl.BlockSpec(memory_space=pl.ANY),
+            pl.BlockSpec(memory_space=pl.ANY),
+        ],
+        out_specs=pl.BlockSpec(memory_space=pltpu.VMEM),
+        scratch_shapes=[
+            pltpu.VMEM(text_kv.shape, bf16),
+            pltpu.VMEM(out_weight.shape, bf16),
+            pltpu.VMEM((groups, rows, width), bf16),
+            pltpu.VMEM((groups, rows, width), bf16),
+            pltpu.VMEM((seq, groups, rows, width), bf16),
+            pltpu.VMEM((seq, groups, rows, cols), bf16),
+            pltpu.VMEM((seq, n_head, rows, cols), bf16),
+            pltpu.VMEM((seq, rows, cols), bf16),
+            pltpu.VMEM((seq, rows, cols), bf16),
+            pltpu.VMEM((seq, rows, cols), bf16),
+            dma((3,)),
+            dma((groups,)),
+            dma((groups,)),
+            dma((2, seq, groups)),
+            dma((2, seq, groups)),
+            dma((seq, 2)),
+            dma((seq, 2)),
+            dma((seq,)),
+            dma((seq,)),
+            dma((seq,)),
+            dma((seq,)),
+        ],
+        compiler_params=pltpu.CompilerParams(
+            collective_id=0, has_side_effects=True, vmem_limit_bytes=56 * 2**20
+        ),
+    )(q_mant, q_exp, lengths, text_kv, out_weight)
+
+
+def fits(mesh, q_mant, q_exp, text_kv, out_weight, lengths):
+    if (mesh.shape["seq"], mesh.shape["head"], mesh.shape["sub"]) != (4, 2, 2):
+        return False
+    head_size = q_mant.shape[1] // q_exp.shape[1]
+    return (
+        head_size == 128
+        and q_mant.shape[0] * 4 == FRAME_TOK
+        and q_mant.shape[0] % 16 == 0
+        and (out_weight.shape[0] // head_size) % UNROLL == 0
+        and out_weight.shape[1] % BLOCK == 0
+    )
 
 
 def shards(q_mant, q_exp, text_kv, out_weight, lengths):
@@ -63,8 +389,11 @@
 
 
 def solution(mesh):
+    def step(*arrays):
+        return fused(mesh, *arrays) if fits(mesh, *arrays) else shards(*arrays)
+
     return jax.shard_map(
-        shards,
+        step,
         mesh=mesh,
         in_specs=(
             P(("grp", "seq", "head", "sub"), None),

time: 123 us -> 54 us (0.44)
  waiting for transfers between devices: 66.9 us -> 0 us
  Pallas kernels: 0 us -> 52 us
  blocking collectives: 16.3 us -> 0 us
  between operations: 13.5 us -> 0.01 us
  local copies, waits for them, and re-layouts: 10.9 us -> 1.77 us
  matrix products: 6.68 us -> 0 us
  starting transfers between devices: 4.25 us -> 0 us
  other arithmetic: 3.72 us -> 0 us
    pallas_call x0 -> x1, Pallas kernels: none -> 52 us  [fused(): pl.pallas_call(functools.partial(kernel, (seq, n_head, n_sub, q_exp.shape...]
    all_gather x1 -> x0, waiting for transfers between devices: 39 us -> none  [shards(): gathered = lax.all_gather(attended, 'seq', axis=0, tiled=False)]
    reduce_scatter x1 -> x0, waiting for transfers between devices: 27.2 us -> none  [shards(): lax.psum_scatter(term.reshape(groups * seq * tok_dev, cols), ('head', 'su...]
    all_to_all x1 -> x0, blocking collectives: 16.3 us -> none  [shards(): lax.all_to_all(summed.reshape(seq, tok_dev, cols), 'seq', split_axis=0, c...]
    dot_general x3 -> x0, matrix products: 6.68 us -> none  [the longest x1 5.41 us: shards(): jnp.dot(gathered.reshape(seq * rows, -1), out_weight, preferred_element_t...]
    slice x2 -> x0, local copies, waits for them, and re-layouts: 4.84 us -> none  [the longest x1 3.24 us: shards(): keys = text_kv[0].reshape(-1, local_heads, head_size)]
    all_to_all x1 -> x0, starting transfers between devices: 4.21 us -> none  [shards(): lax.all_to_all(query.reshape(q_mant.shape), ('head', 'sub'), split_axis=1...]
    reshape x3 -> x0, local copies, waits for them, and re-layouts: 2.34 us -> none  [the longest x1 1.29 us: shards(): term = term.reshape(seq, groups, tok_dev, cols).transpose(1, 0, 2, 3)]
  transfers between devices with their start and end apart: 3 -> 0, of which waited for: 3 -> 0; matrix products, arithmetic and copies ran while one was open for 6% -> 0% of each run, Pallas kernels for 0% -> 0%
where the time goes in v3:
time: 54 us; the launch traced here: 53.8 us
  Pallas kernels  52 us (96%)
  local copies, waits for them, and re-layouts  1.77 us (3%)
    pallas_call x1, Pallas kernels, fused(): pl.pallas_call(functools.partial(kernel, (seq, n_head, n_sub, q_exp.shape...  52 us
    unnamed x1, local copies, waits for them, and re-layouts  1.77 us

profile of v3, /device:TPU:0, one launch (start us, length us, event | category | flops | bytes accessed | tf_op | source)
XLA Modules:
  0.0 53.8 jit_solution(5768258827453565510)
XLA Ops:
  0.0 52.0 %shard_map.55 = bf16[32,6144]{1,0:T(8,128)(2,1)} custom-call(bf16[32,6144]{1,0:T(8,128)(2,1)} %q_ref.1, s32[32,48]{1,0:T(8,128)} %e_ref.1, s32[4]{0:T(128)} %len_ref.1, bf16[2,512,1536]{2,1,0:T(8,128)(2,1)} %kv_ref.1, bf16[1536,1536]{1,0:T(8,128)(2,1)} %w_ref.1), custom_call_target="tpu_custom_call" | custom-call | tf_op jit(solution)/shard_map/pallas_call | solution.py:282
  52.1 1.8 %copy.7 = bf16[32,6144]{1,0:T(8,128)(2,1)} copy(bf16[32,6144]{1,0:T(8,128)(2,1)} %shard_map.55) | data formatting | bytes 786432

commit v4 on v3

--- a/solution.py
+++ b/solution.py
@@ -11,7 +11,7 @@
 FRAME_TOK = 128
 MESH = pl.DeviceIdType.MESH
 BLOCK = 512
-UNROLL = 4
+UNROLL = 12
 
 
 def kernel(
@@ -118,18 +118,27 @@
 
     def attend(d):
         def some(i, carry):
-            for extra in range(UNROLL):
-                lanes = pl.ds(pl.multiple_of((i * UNROLL + extra) * head_size, head_size), head_size)
-                scores = lax.dot_general(
-                    qr[d, :, lanes], kv[0, :, lanes], (((1,), (1,)), ((), ())),
+            lanes = [
+                pl.ds(pl.multiple_of((i * UNROLL + extra) * head_size, head_size), head_size)
+                for extra in range(UNROLL)
+            ]
+            scores = [
+                lax.dot_general(
+                    qr[d, :, one], kv[0, :, one], (((1,), (1,)), ((), ())),
                     preferred_element_type=f32,
                 )
-                scores = jnp.where(valid, scores, -1e30)
-                top = jnp.max(scores, axis=1, keepdims=True)
-                probs = jnp.exp2((scores - top) * scale)
-                total = jnp.sum(probs, axis=1, keepdims=True)
-                mixed = jnp.dot(probs.astype(bf16), kv[1, :, lanes], preferred_element_type=f32)
-                att[z, d, :, lanes] = (mixed * (1.0 / total)).astype(bf16)
+                for one in lanes
+            ]
+            scores = [jnp.where(valid, one, -1e30) for one in scores]
+            tops = [jnp.max(one, axis=1, keepdims=True) for one in scores]
+            probs = [jnp.exp2((one - top) * scale) for one, top in zip(scores, tops)]
+            totals = [jnp.sum(one, axis=1, keepdims=True) for one in probs]
+            mixed = [
+                jnp.dot(prob.astype(bf16), kv[1, :, one], preferred_element_type=f32)
+                for prob, one in zip(probs, lanes)
+            ]
+            for one, value, total in zip(lanes, mixed, totals):
+                att[z, d, :, one] = (value * (1.0 / total)).astype(bf16)
             return carry
 
         lax.fori_loop(0, local_heads // UNROLL, some, 0)

time: 54 us -> 50.4 us (0.933)
  Pallas kernels: 52 us -> 48.5 us
    pallas_call x1, Pallas kernels: 52 us -> 48.5 us  [fused(): pl.pallas_call(functools.partial(kernel, (seq, n_head, n_sub, q_exp.shape...]
where the time goes in v4:
time: 50.4 us; the launch traced here: 50.3 us
  Pallas kernels  48.5 us (96%)
  local copies, waits for them, and re-layouts  1.77 us (4%)
    pallas_call x1, Pallas kernels, fused(): pl.pallas_call(functools.partial(kernel, (seq, n_head, n_sub, q_exp.shape...  48.5 us
    unnamed x1, local copies, waits for them, and re-layouts  1.77 us

profile of v4, /device:TPU:0, one launch (start us, length us, event | category | flops | bytes accessed | tf_op | source)
XLA Modules:
  0.0 50.3 jit_solution(9174535269162999359)
XLA Ops:
  0.0 48.5 %shard_map.55 = bf16[32,6144]{1,0:T(8,128)(2,1)} custom-call(bf16[32,6144]{1,0:T(8,128)(2,1)} %q_ref.1, s32[32,48]{1,0:T(8,128)} %e_ref.1, s32[4]{0:T(128)} %len_ref.1, bf16[2,512,1536]{2,1,0:T(8,128)(2,1)} %kv_ref.1, bf16[1536,1536]{1,0:T(8,128)(2,1)} %w_ref.1), custom_call_target="tpu_custom_call" | custom-call | tf_op jit(solution)/shard_map/pallas_call | solution.py:291
  48.5 1.8 %copy.7 = bf16[32,6144]{1,0:T(8,128)(2,1)} copy(bf16[32,6144]{1,0:T(8,128)(2,1)} %shard_map.55) | data formatting | bytes 786432

commit v5 on v4

--- a/solution.py
+++ b/solution.py
@@ -237,19 +237,19 @@
     pair(1)
     for d in (2, 3, 0, 1):
         arrive(2, d)
-    finish(1)
     project(2, 0, 4)
     pair(2)
-    finish(2)
     arrive(3, 2)
     arrive(3, 3)
     project(3, 2, 2)
     pair(3)
+    finish(1)
+    finish(2)
     arrive(3, 0)
     arrive(3, 1)
     project(3, 0, 2)
+    finish(3)
     finish(0)
-    finish(3)
 
     for source in range(seq):
 

time: 50.4 us -> 46.6 us (0.925)
  Pallas kernels: 48.5 us -> 44.7 us
    pallas_call x1, Pallas kernels: 48.5 us -> 44.7 us  [fused(): pl.pallas_call(functools.partial(kernel, (seq, n_head, n_sub, q_exp.shape...]
where the time goes in v5:
time: 46.6 us; the launch traced here: 46.5 us
  Pallas kernels  44.7 us (96%)
  local copies, waits for them, and re-layouts  1.77 us (4%)
    pallas_call x1, Pallas kernels, fused(): pl.pallas_call(functools.partial(kernel, (seq, n_head, n_sub, q_exp.shape...  44.7 us
    unnamed x1, local copies, waits for them, and re-layouts  1.77 us

profile of v5, /device:TPU:0, one launch (start us, length us, event | category | flops | bytes accessed | tf_op | source)
XLA Modules:
  0.0 46.5 jit_solution(10763091875278116391)
XLA Ops:
  0.0 44.7 %shard_map.55 = bf16[32,6144]{1,0:T(8,128)(2,1)} custom-call(bf16[32,6144]{1,0:T(8,128)(2,1)} %q_ref.1, s32[32,48]{1,0:T(8,128)} %e_ref.1, s32[4]{0:T(128)} %len_ref.1, bf16[2,512,1536]{2,1,0:T(8,128)(2,1)} %kv_ref.1, bf16[1536,1536]{1,0:T(8,128)(2,1)} %w_ref.1), custom_call_target="tpu_custom_call" | custom-call | tf_op jit(solution)/shard_map/pallas_call | solution.py:291
  44.7 1.8 %copy.7 = bf16[32,6144]{1,0:T(8,128)(2,1)} copy(bf16[32,6144]{1,0:T(8,128)(2,1)} %shard_map.55) | data formatting | bytes 786432
